TPU v7x, 1024 devices: a whole 4x8x16 slice. The times are simulated.
1024 devices in a mesh: expert: 16 (over z), tensor: 64 (over y, x, core).
Axes of the slice: x: 4, y: 8, z: 16, core: 2. Of those that a mesh axis runs over, the one named last changes fastest.
Arguments:
- tokens: bfloat16 [192, 6144], P('expert', 'tensor'), may hold values from -6 to 6
- out_grad: bfloat16 [192, 6144], P('expert', 'tensor'), may hold values from -1.5 to 1.5
- expert_ids: int32 [192, 4], P('expert'), may hold values from 0 to 7, all different within a row; in each aligned block of 12 rows (0 to 11, 12 to 23, ...) at most 10 rows name the same one
- gate_probs: float32 [192, 4], P('expert'), may hold values from 0.05 to 1
- w_gate: bfloat16 [16, 5376, 6144], P('expert', 'tensor'), may hold values from -0.21875 to 0.21875
- w_up: bfloat16 [16, 5376, 6144], P('expert', 'tensor'), may hold values from -0.21875 to 0.21875
- w_down: bfloat16 [16, 5376, 6144], P('expert', 'tensor'), may hold values from -0.0625 to 0.0625
Outputs:
- token_grad: bfloat16 [192, 6144], P('expert', 'tensor')
- gate_grad: float32 [192, 4], P('expert')
Inputs may be any that keep to these rules, and one draw needn't show every extreme that they name: `expert_ids`: each token names 4 different experts. In the rows of one device (aligned blocks of 12 tokens) no expert is named more than 10 times, a bound that some block reaches.
All inputs are finite; a program needn't handle non-finite values.
Results may differ from a plain program's by a relative error of at most 0.011.
Values may be sent and summed in bfloat16 or wider, within the bound.
A program may use at most 32 MiB of HBM per device.

v0:
```python
import jax
import jax.numpy as jnp
from jax import lax
from jax.sharding import PartitionSpec as P

D = 6144
FF = 10752


def silu_parts(pre_gate):
    sigmoid_val = jax.nn.sigmoid(pre_gate)
    return (pre_gate * sigmoid_val, sigmoid_val * (1.0 + pre_gate * (1.0 - sigmoid_val)))


def body(tokens, out_grad, expert_ids, gate_probs, w_gate, w_up, w_down):
    n_expert = lax.axis_size("expert")
    n_tensor = lax.axis_size("tensor")
    tok_rows, choose_count = expert_ids.shape
    half_width = w_gate.shape[1]
    half_count = FF // (half_width * n_tensor)
    n_experts = n_expert // half_count
    slot_count = min(tok_rows, tok_rows * choose_count * 5 // (n_experts * 3))
    row_count = n_expert * slot_count
    feature_width = D // n_tensor
    flat_ids = expert_ids.reshape(-1)
    onehot = (flat_ids[:, None] == jnp.arange(n_experts, dtype=jnp.int32)[None, :]).astype(
        jnp.int32
    )
    position_in = jnp.sum((jnp.cumsum(onehot, axis=0) - 1) * onehot, axis=1)
    slot_index = flat_ids * slot_count + position_in
    placed = (
        slot_index[:, None] == jnp.arange(n_experts * slot_count, dtype=jnp.int32)[None, :]
    ).astype(jnp.float32)
    placed = placed.reshape(tok_rows, choose_count, n_experts * slot_count)
    route_table = jnp.sum(placed, axis=1).reshape(tok_rows, n_experts, slot_count)
    spread = jnp.repeat(route_table, half_count, axis=1).astype(jnp.bfloat16)
    gate_matrix = w_gate[0]
    up_matrix = w_up[0]
    down_matrix = w_down[0]
    send_rows = jnp.einsum(
        "tjs,tf->jsf", spread, tokens, preferred_element_type=jnp.float32
    ).astype(jnp.bfloat16)
    send_grad = jnp.einsum(
        "tjs,tf->jsf", spread, out_grad, preferred_element_type=jnp.float32
    ).astype(jnp.bfloat16)
    got_rows, got_grad = (
        lax.all_to_all(send_rows, "expert", split_axis=0, concat_axis=0, tiled=True),
        lax.all_to_all(send_grad, "expert", split_axis=0, concat_axis=0, tiled=True),
    )
    got_rows = got_rows.reshape(row_count, feature_width)
    got_grad = got_grad.reshape(row_count, feature_width)
    row_piece = lax.all_gather(got_rows, "tensor", axis=1, tiled=True)
    grad_piece = lax.all_gather(got_grad, "tensor", axis=1, tiled=True)
    gate_cols = gate_matrix
    up_cols = up_matrix
    contract = (((1,), (1,)), ((), ()))
    gate_acc = lax.dot_general(row_piece, gate_cols, contract, preferred_element_type=jnp.float32)
    up_acc = lax.dot_general(row_piece, up_cols, contract, preferred_element_type=jnp.float32)
    back_acc = lax.dot_general(
        grad_piece, down_matrix, contract, preferred_element_type=jnp.float32
    )
    activated, slope_term = silu_parts(gate_acc)
    hidden = (activated * up_acc).astype(jnp.bfloat16)
    gate_terms = jnp.sum(hidden.astype(jnp.float32) * back_acc, axis=1)
    grad_gate = (back_acc * up_acc * slope_term).astype(jnp.bfloat16)
    grad_up = (back_acc * activated).astype(jnp.bfloat16)
    gate_cols = gate_matrix
    up_cols = up_matrix
    contract = (((0,), (1,)), ((), ()))
    term = lax.dot_general(gate_cols, grad_gate, contract, preferred_element_type=jnp.float32)
    feature_part = lax.psum_scatter(
        term + lax.dot_general(up_cols, grad_up, contract, preferred_element_type=jnp.float32),
        "tensor",
        scatter_dimension=0,
        tiled=True,
    )
    gate_sum = lax.psum(gate_terms, "tensor")
    back_rows = feature_part.T.reshape(n_expert, slot_count, feature_width)
    back_gate = gate_sum.reshape(n_expert, slot_count)
    returned_rows, returned_gate = (
        lax.all_to_all(
            back_rows.astype(jnp.bfloat16), "expert", split_axis=0, concat_axis=0, tiled=True
        ).astype(back_rows.dtype),
        lax.all_to_all(
            back_gate.astype(jnp.bfloat16), "expert", split_axis=0, concat_axis=0, tiled=True
        ).astype(back_gate.dtype),
    )
    summed_rows = jnp.sum(
        returned_rows.reshape(n_experts, half_count, slot_count, feature_width), axis=1
    )
    summed_rows = summed_rows.reshape(n_experts * slot_count, feature_width)
    summed_gate = jnp.sum(returned_gate.reshape(n_experts, half_count, slot_count), axis=1).reshape(
        -1
    )
    weighted = jnp.sum(placed * gate_probs[:, :, None], axis=1)
    token_grad = jnp.dot(weighted, summed_rows, precision=lax.Precision.HIGHEST).astype(
        jnp.bfloat16
    )
    gate_grad = jnp.einsum("tks,s->tk", placed, summed_gate, precision=lax.Precision.HIGHEST)
    return (token_grad, gate_grad)


def solution(mesh):
    in_specs = (
        P("expert", "tensor"),
        P("expert", "tensor"),
        P("expert", None),
        P("expert", None),
        P("expert", "tensor", None),
        P("expert", "tensor", None),
        P("expert", "tensor", None),
    )
    out_specs = (P("expert", "tensor"), P("expert", None))
    return jax.shard_map(body, mesh=mesh, in_specs=in_specs, out_specs=out_specs, check_vma=False)
```

profile of v0, /device:TPU:6, one launch (start us, length us, event | category | flops | bytes accessed | tf_op | source)
XLA Modules:
  0.0 452.1 jit_solution(9995703392303214613)
XLA Ops:
  7.2 0.9 copy.29
  8.2 0.8 copy.31
  9.8 0.8 convolution_convert_fusion
  10.7 31.2 %all_to_all.21 = bf16[16,2,480]{2,1,0:T(2,128)(2,1)S(1)} all-to-all(bf16[16,2,480]{2,1,0:T(2,128)(2,1)S(1)} %reshape.108), channel_id=1, replica_groups=mesh['expert'=16,'tensor'=64] {'expert'}, dimensions={0} | all-to-all | bytes 61440 | tf_op jit(solution)/shard_map/all_to_all | solution.py:47
  42.8 0.8 convolution_convert_fusion.1
  43.8 15.2 %all_to_all.22 = bf16[16,2,480]{2,1,0:T(2,128)(2,1)S(1)} all-to-all(bf16[16,2,480]{2,1,0:T(2,128)(2,1)S(1)} %reshape.110), channel_id=1, replica_groups=mesh['expert'=16,'tensor'=64] {'expert'}, dimensions={0} | all-to-all | bytes 61440 | tf_op jit(solution)/shard_map/all_to_all | solution.py:48
  59.8 67.1 %all-gather.7.cloned.1.call-done = bf16[64,96,160]{1,2,0:T(8,128)(2,1)} async-done(((bf16[1,96,160]{1,2,0:T(8,128)(2,1)}), bf16[64,96,160]{1,2,0:T(8,128)(2,1)}) %all-gather.7.cloned.1.call-update) | async-done | bytes 1966096 | tf_op jit(solution)/shard_map/all_gather | solution.py:52
  126.9 4.3 copy.36
  131.1 5.0 %reshape.100 = bf16[6144,160]{0,1:T(8,128)(2,1)S(1)} reshape(bf16[64,96,160]{1,0,2:T(8,128)(2,1)} %copy.36) | data formatting | bytes 3932160
  136.1 87.2 %all-gather.5.cloned.1.call-done = bf16[64,96,160]{1,2,0:T(8,128)(2,1)} async-done(((bf16[1,96,160]{1,2,0:T(8,128)(2,1)}), bf16[64,96,160]{1,2,0:T(8,128)(2,1)}) %all-gather.5.cloned.1.call-update) | async-done | bytes 1966096 | tf_op jit(solution)/shard_map/all_gather | solution.py:53
  223.3 4.3 copy.34
  227.6 6.0 %reshape.98 = bf16[6144,160]{0,1:T(8,128)(2,1)} reshape(bf16[64,96,160]{1,0,2:T(8,128)(2,1)} %copy.34) | data formatting | bytes 3932160
  235.5 0.8 copy-done.1
  236.7 0.8 multiply_reduce_fusion
  238.1 2.6 fusion
  240.8 6.0 %copy.40 = f32[6144,160]{1,0:T(8,128)} copy(f32[6144,160]{0,1:T(8,128)} %fusion) | data formatting | bytes 7864320
  246.8 113.1 %psum.7 = bf16[160]{0:T(256)(128)(2,1)S(1)} all-reduce(f32[160]{0:T(256)S(1)} %get-tuple-element.4), channel_id=1, replica_groups=mesh['expert'=16,'tensor'=64] {'tensor'}, use_global_device_ids=true, to_apply=%region_7.8 | all-reduce | flops 160 | bytes 960 | tf_op jit(solution)/shard_map/psum | solution.py:77
  360.6 13.0 %all-to-all-start.3 = ((bf16[16,1,10]{2,1,0:T(2,128)(2,1)}), bf16[16,1,10]{2,1,0:T(2,128)(2,1)S(1)}, u32[]{:S(2)}, u32[]{:S(2)}) async-start(bf16[16,1,10]{2,1,0:T(2,128)(2,1)} %convert_element_type.92), calls=%async_computation.3 | async-start | bytes 16384 | tf_op jit(solution)/shard_map/all_to_all | solution.py:84
  373.7 12.2 %all-to-all-done.3 = bf16[16,1,10]{2,1,0:T(2,128)(2,1)S(1)} async-done(((bf16[16,1,10]{2,1,0:T(2,128)(2,1)}), bf16[16,1,10]{2,1,0:T(2,128)(2,1)S(1)}, u32[]{:S(2)}, u32[]{:S(2)}) %all-to-all-start.3) | async-done | bytes 352 | tf_op jit(solution)/shard_map/all_to_all | solution.py:84
  386.0 31.5 %reduce-scatter.4.cloned.1.call-done = f32[96,160]{1,0:T(8,128)} async-done(((f32[6144,160]{1,0:T(8,128)}), f32[96,160]{1,0:T(8,128)}) %reduce-scatter.4.cloned.1.call-update) | async-done | bytes 61456
  417.4 1.0 copy.41
  419.2 12.9 %all-to-all-start.2 = ((bf16[16,2,480]{2,1,0:T(2,128)(2,1)}), bf16[16,2,480]{2,1,0:T(2,128)(2,1)S(1)}, u32[]{:S(2)}, u32[]{:S(2)}) async-start(bf16[16,2,480]{2,1,0:T(2,128)(2,1)} %reshape.112), calls=%async_computation.2 | async-start | bytes 65536 | tf_op jit(solution)/shard_map/all_to_all | solution.py:81
  432.1 0.8 fusion.12
  432.9 11.8 %all-to-all-done.2 = bf16[16,2,480]{2,1,0:T(2,128)(2,1)S(1)} async-done(((bf16[16,2,480]{2,1,0:T(2,128)(2,1)}), bf16[16,2,480]{2,1,0:T(2,128)(2,1)S(1)}, u32[]{:S(2)}, u32[]{:S(2)}) %all-to-all-start.2) | async-done | bytes 30752 | tf_op jit(solution)/shard_map/all_to_all | solution.py:81
  (45 shorter events, 8.3 us)
Async XLA Ops:
  7.2 226.4 %copy-start = (bf16[1,84,6144]{2,1,0:T(8,128)(2,1)S(1)}, bf16[1,84,6144]{2,1,0:T(8,128)(2,1)}, u32[]{:S(2)}) copy-start(bf16[1,84,6144]{2,1,0:T(8,128)(2,1)} %param.11) | copy-start | bytes 3096580
  7.2 119.7 %all-gather.7.cloned.1.call-start = ((), (), s32[]{:S(2)}) async-start(), calls=%async_computation.6 | async-start | bytes 2662400 | tf_op jit(solution)/shard_map/all_gather | solution.py:52
  42.7 180.6 %all-gather.5.cloned.1.call-start = ((), (), s32[]{:S(2)}) async-start(), calls=%async_computation.5 | async-start | bytes 2662400 | tf_op jit(solution)/shard_map/all_gather | solution.py:53
  59.7 357.7 %reduce-scatter.4.cloned.1.call-start = ((), (), s32[]{:S(2)}) async-start(), calls=%async_computation.7 | async-start | bytes 6389760
  233.6 1.2 copy-start.2
  234.8 1.5 copy-start.1
  234.8 1.8 copy-start.3
  360.6 25.3 %all-to-all-start.3 = ((bf16[16,1,10]{2,1,0:T(2,128)(2,1)}), bf16[16,1,10]{2,1,0:T(2,128)(2,1)S(1)}, u32[]{:S(2)}, u32[]{:S(2)}) async-start(bf16[16,1,10]{2,1,0:T(2,128)(2,1)} %convert_element_type.92), calls=%async_computation.3 | async-start | bytes 16384 | tf_op jit(solution)/shard_map/all_to_all | solution.py:84
  419.2 25.5 %all-to-all-start.2 = ((bf16[16,2,480]{2,1,0:T(2,128)(2,1)}), bf16[16,2,480]{2,1,0:T(2,128)(2,1)S(1)}, u32[]{:S(2)}, u32[]{:S(2)}) async-start(bf16[16,2,480]{2,1,0:T(2,128)(2,1)} %reshape.112), calls=%async_computation.2 | async-start | bytes 65536 | tf_op jit(solution)/shard_map/all_to_all | solution.py:81
Sparse Core Ops, SparseCore 0:
  42.9 83.9 all-gather.6
  131.3 91.9 all-gather.4
  246.9 170.4 reduce-scatter.3
where the time goes:
time: 454 us; the launch traced here: 452 us
  waiting for transfers between devices  210 us (46%)
  blocking collectives  159 us (35%)
  local copies, waits for them, and re-layouts  33.7 us (7%)
  starting transfers between devices  26 us (6%)
  between operations  13.9 us (3%)
  matrix products  8.65 us (2%)
    psum x1, blocking collectives, body(): gate_sum = lax.psum(gate_terms, 'tensor')  113 us
    all_gather x1, waiting for transfers between devices, body(): grad_piece = lax.all_gather(got_grad, 'tensor', axis=1, tiled=True)  87.2 us
    all_gather x1, waiting for transfers between devices, body(): row_piece = lax.all_gather(got_rows, 'tensor', axis=1, tiled=True)  67.1 us
    unnamed x4, waiting for transfers between devices  31.5 us
    all_to_all x1, blocking collectives, body(): lax.all_to_all(send_rows, 'expert', split_axis=0, concat_axis=0, tiled=True)  31.2 us
    unnamed x20, local copies, waits for them, and re-layouts  22.6 us
    all_to_all x1, blocking collectives, body(): lax.all_to_all(send_grad, 'expert', split_axis=0, concat_axis=0, tiled=True)  15.2 us
    all_to_all x1, starting transfers between devices, body(): lax.all_to_all(back_gate.astype(jnp.bfloat16), 'expert', split_axis=0, co...  13 us
  transfers between devices with their start and end apart: 5, of which 5 were waited for; matrix products, arithmetic and copies ran while one was open for 3% of the time, Pallas kernels for 0%

commit v1 on v0

v1 whole, which is shorter than its diff:
```python
import jax
import jax.numpy as jnp
from jax import lax
from jax.experimental import pallas as pl
from jax.experimental.pallas import tpu as pltpu
from jax.sharding import PartitionSpec as P

MESH = pl.DeviceIdType.MESH
BF = jnp.bfloat16
F32 = jnp.float32
NZ, NY, NX = 16, 8, 4
SLICES = NY * NX
HID = 84
HPAD = 96
FEAT = 96
LANE = 128
TOK = 12
ROWS = NZ * TOK
COLS = 2 * ROWS
WIDE = NY * LANE


def iota(shape, dim):
    return lax.broadcasted_iota(jnp.int32, shape, dim)


def dot(a, b, ca=1, cb=0):
    return lax.dot_general(a, b, (((ca,), (cb,)), ((), ())), preferred_element_type=F32)


def kernel(
    tok, grad, ids, probs, wg, wu, wd,
    tg_out, gg_out,
    wraw, wr, wall, zsend, zbuf, xbuf, part, part2, gcat,
    xs, xr, ysend, yrecv, rsend, rrecv,
    wsem, lsem, ssem, csem,
    zss, zrs, xss, xrs, yss, yrs, rxs, rxr, rys, ryr, rzs, rzr,
):
    z = lax.axis_index("expert")
    t = lax.axis_index("tensor")
    y = t // 8
    x = lax.rem(t // 2, 4)
    c = lax.rem(t, 2)
    other = 1 - c

    def dev(zz, yy, xx, cc):
        return (zz, (yy * NX + xx) * 2 + cc)

    def zdev(d):
        return dev(lax.rem(z + d, NZ), y, x, c)

    def ydev(d):
        return dev(z, lax.rem(y + d, NY), x, c)

    def xdev(d):
        return dev(z, y, lax.rem(x + d, NX), c)

    sibling = dev(z, y, x, other)

    def remote(src, dst, ss, rs, target):
        return pltpu.make_async_remote_copy(
            src_ref=src, dst_ref=dst, send_sem=ss, recv_sem=rs, device_id=target, device_id_type=MESH
        )

    bar = pltpu.get_barrier_semaphore()

    def greet_z(d, carry):
        pl.semaphore_signal(bar, inc=1, device_id=zdev(d), device_id_type=MESH)
        return carry

    def greet_y(d, carry):
        pl.semaphore_signal(bar, inc=1, device_id=ydev(d), device_id_type=MESH)
        return carry

    def greet_x(d, carry):
        pl.semaphore_signal(bar, inc=1, device_id=xdev(d), device_id_type=MESH)
        return carry

    lax.fori_loop(1, NZ, greet_z, 0)
    lax.fori_loop(1, NY, greet_y, 0)
    lax.fori_loop(1, NX, greet_x, 0)
    pl.semaphore_signal(bar, inc=1, device_id=sibling, device_id_type=MESH)

    loads = [
        pltpu.make_async_copy(src.at[0], wraw.at[i], wsem.at[i]) for i, src in enumerate((wg, wu, wd))
    ]
    for cp in loads:
        cp.start()

    zsend[...] = jnp.zeros_like(zsend)
    zsend[0:TOK, 0:FEAT] = tok[...]
    zsend[16:16 + TOK, 0:FEAT] = grad[...]
    zbuf[z] = zsend[...]

    pl.semaphore_wait(bar, (NZ - 1) + (NY - 1) + (NX - 1) + 1)

    def zcopy(d):
        return remote(zsend, zbuf.at[z], zss.at[d], zrs.at[d], zdev(d))

    def zstart(i, carry):
        zcopy(lax.rem(i + 7, 15) + 1).start()
        return carry

    lax.fori_loop(0, NZ - 1, zstart, 0)

    xbuf[:, FEAT:LANE, :] = jnp.zeros((SLICES, LANE - FEAT, COLS), BF)
    wr[:, :, 80:HPAD, :] = jnp.zeros((2, 3, HPAD - 80, SLICES * LANE), BF)
    row = iota((4 * FEAT, 4 * LANE), 0)
    q = (
        (row >= FEAT).astype(jnp.int32)
        + (row >= 2 * FEAT).astype(jnp.int32)
        + (row >= 3 * FEAT).astype(jnp.int32)
    )
    spread = jnp.where(iota((4 * FEAT, 4 * LANE), 1) == row + q * (LANE - FEAT), 1.0, 0.0).astype(BF)
    for cp in loads:
        cp.wait()

    def relay(g, carry):
        yy = g // 2
        xx = 2 * lax.rem(g, 2)
        for i in range(3):
            wide = dot(
                wraw[i, :, pl.ds(pl.multiple_of(g * (4 * FEAT), LANE), 4 * FEAT)], spread
            ).astype(BF)
            for j in range(4):
                at = pl.multiple_of(((xx + j // 2) * NY + yy) * LANE, LANE)
                wr[j % 2, i, 0:HID, pl.ds(at, LANE)] = wide[:, j * LANE:(j + 1) * LANE]
        return carry

    lax.fori_loop(0, 16, relay, 0)
    wsend = remote(wr.at[other], wall.at[:, c], ssem.at[0], ssem.at[1], sibling)
    wsend.start()
    wown = pltpu.make_async_copy(wr.at[c], wall.at[:, c], lsem.at[0])
    wown.start()

    def zwait(d, carry):
        zcopy(d).wait_recv()
        return carry

    lax.fori_loop(1, NZ, zwait, 0)
    r = iota((NZ * 32, COLS), 0)
    col = iota((NZ * 32, COLS), 1)
    want = ((r >> 4) & 1) * ROWS + (r >> 5) * TOK + (r & 15)
    pick = jnp.where((col == want) & ((r & 15) < TOK), 1.0, 0.0).astype(BF)
    mine = dot(zbuf[...].reshape(NZ * 32, LANE), pick, 0, 0).astype(BF)
    slot = x * NY + y
    xbuf[slot, 0:FEAT, :] = mine[0:FEAT, :]

    def xcopy(d):
        return remote(
            xbuf.at[slot, pl.ds(0, FEAT)], xbuf.at[slot, pl.ds(0, FEAT)], xss.at[d], xrs.at[d], xdev(d)
        )

    for d in (2, 1, 3):
        xcopy(d).start()

    half = FEAT // 2

    def ycopy(i, s, way):
        xx = lax.rem(x + NX - i, NX)
        yy = lax.rem(y + NY - s, NY) if way == 0 else lax.rem(y + s, NY)
        rows = pl.ds(0, FEAT) if s < 3 else pl.ds(way * half, half)
        ref = xbuf.at[xx * NY + yy, rows]
        return remote(ref, ref, yss.at[way, i, s], yrs.at[way, i, s], ydev(1 if way == 0 else NY - 1))

    for i in (0, 1, 3, 2):
        if i:
            xcopy(i).wait_recv()
        ycopy(i, 0, 0).start()
        ycopy(i, 0, 1).start()
    for s in (1, 2, 3):
        for i in (0, 1, 3, 2):
            for way in (0, 1):
                ycopy(i, s - 1, way).wait_recv()
                ycopy(i, s, way).start()
    for i in (0, 1, 3, 2):
        for way in (0, 1):
            ycopy(i, 3, way).wait_recv()

    wown.wait()
    wsend.wait_recv()
    part[...] = jnp.zeros_like(part)

    def forward(k, carry):
        lanes = pl.ds(pl.multiple_of(k * WIDE, LANE), WIDE)
        blk = xbuf[pl.ds(k * NY, NY)].reshape(WIDE, COLS)
        both = wall[0:2, :, :, lanes].reshape(4 * HPAD, WIDE)
        part[0:2] += dot(both, blk[:, 0:256]).reshape(2, 2 * HPAD, 256)
        part[2] += dot(wall[2, :, :, lanes].reshape(2 * HPAD, WIDE), blk[:, 128:384])
        return carry

    lax.fori_loop(0, NX, forward, 0)
    psend = remote(part, part2, csem.at[0], csem.at[1], sibling)
    psend.start()
    psend.wait()
    pre_gate = (part[0] + part2[0])[:, 0:ROWS]
    pre_up = (part[1] + part2[1])[:, 0:ROWS]
    back = (part[2] + part2[2])[:, 64:64 + ROWS]
    sig = jax.nn.sigmoid(pre_gate)
    act = pre_gate * sig
    slope = sig * (1.0 + pre_gate * (1.0 - sig))
    hidden = (act * pre_up).astype(BF).astype(F32)
    terms = jnp.sum(hidden * back, axis=0, keepdims=True)
    gcat[0:2 * HPAD, :] = (back * pre_up * slope).astype(BF)
    gcat[2 * HPAD:4 * HPAD, :] = (back * act).astype(BF)

    def gate_lanes(column, rows):
        hi = column.astype(BF).astype(F32)
        lane = iota((rows, LANE), 1)
        return jnp.where(lane == FEAT, hi, jnp.where(lane == FEAT + 1, column - hi, 0.0))

    eye = iota((ROWS, ROWS), 0) == iota((ROWS, ROWS), 1)
    column = jnp.sum(jnp.where(eye, terms, 0.0), axis=1, keepdims=True)
    ride = gate_lanes(column, ROWS)
    ride = jnp.concatenate([ride] * NY, axis=1)

    gt = gcat[...]

    def block(xx):
        lanes = pl.ds(pl.multiple_of(xx * WIDE, LANE), WIDE)
        return dot(gt, wall[0:2, :, :, lanes].reshape(4 * HPAD, WIDE), 0, 0) + ride

    def rxcopy(d):
        return remote(xs.at[d - 1], xr.at[d - 1], rxs.at[d], rxr.at[d], xdev(d))

    for d in (2, 1, 3):
        xs[d - 1] = block(lax.rem(x + d, NX)).astype(BF)
        rxcopy(d).start()
    total = block(x)
    for d in (1, 3, 2):
        rxcopy(d).wait_recv()
        total = total + xr[d - 1].astype(F32)

    def regate(v, rows):
        lane = iota((rows, LANE), 1)
        gate = jnp.sum(
            jnp.where((lane == FEAT) | (lane == FEAT + 1), v, 0.0), axis=1, keepdims=True
        )
        return gate_lanes(gate, rows), lane < FEAT

    ride, body = regate(total[:, 0:LANE], ROWS)
    for i in range(NY):
        ysend[i] = jnp.where(body, total[:, i * LANE:(i + 1) * LANE], ride).astype(BF)

    def rycopy(d):
        return remote(ysend.at[lax.rem(y + d, NY)], yrecv.at[d], rys.at[d], ryr.at[d], ydev(d))

    for d in (4, 3, 5, 2, 6, 1, 7):
        rycopy(d).start()
    acc = ysend[y].astype(F32)
    for d in (1, 7, 2, 6, 3, 5, 4):
        rycopy(d).wait_recv()
        acc = acc + yrecv[d].astype(F32)

    ride, body = regate(acc, ROWS)
    acc = jnp.where(body, acc, ride).astype(BF)
    r = iota((NZ * 16, ROWS), 0)
    place = (iota((NZ * 16, ROWS), 1) == (r >> 4) * TOK + (r & 15)) & ((r & 15) < TOK)
    rsend[...] = dot(jnp.where(place, 1.0, 0.0).astype(BF), acc).astype(BF).reshape(NZ, 16, LANE)
    rrecv[z] = rsend[z]

    def rzcopy(d):
        return remote(rsend.at[lax.rem(z + d, NZ)], rrecv.at[z], rzs.at[d], rzr.at[d], zdev(d))

    def rzstart(i, carry):
        rzcopy(lax.rem(i + 7, 15) + 1).start()
        return carry

    lax.fori_loop(0, NZ - 1, rzstart, 0)

    def rzwait(d, carry):
        rzcopy(d).wait_recv()
        return carry

    lax.fori_loop(1, NZ, rzwait, 0)
    chosen = ids[...]
    weight = probs[...]
    out = jnp.zeros((TOK, LANE), F32)
    gout = jnp.zeros((TOK, 4), F32)
    for e in range(NZ // 2):
        hit = chosen == e
        w = jnp.sum(jnp.where(hit, weight, 0.0), axis=1, keepdims=True)
        v = rrecv[2 * e].astype(F32) + rrecv[2 * e + 1].astype(F32)
        v = v[0:TOK]
        out = out + w * v
        gate = v[:, FEAT:FEAT + 1] + v[:, FEAT + 1:FEAT + 2]
        gout = gout + jnp.where(hit, gate, 0.0)
    tg_out[...] = out[:, 0:FEAT].astype(BF)
    gg_out[...] = gout

    def zdone(d, carry):
        zcopy(d).wait_send()
        rzcopy(d).wait_send()
        return carry

    lax.fori_loop(1, NZ, zdone, 0)
    wsend.wait_send()
    for d in range(1, NX):
        xcopy(d).wait_send()
        rxcopy(d).wait_send()
    for d in range(1, NY):
        rycopy(d).wait_send()
    for s in range(4):
        for i in range(NX):
            for way in (0, 1):
                ycopy(i, s, way).wait_send()


def body(tokens, out_grad, expert_ids, gate_probs, w_gate, w_up, w_down):
    vmem = pl.BlockSpec(memory_space=pltpu.VMEM)
    hbm = pl.BlockSpec(memory_space=pl.ANY)
    dma = pltpu.SemaphoreType.DMA
    return pl.pallas_call(
        kernel,
        out_shape=(
            jax.ShapeDtypeStruct((TOK, FEAT), BF),
            jax.ShapeDtypeStruct((TOK, 4), F32),
        ),
        in_specs=[vmem, vmem, vmem, vmem, hbm, hbm, hbm],
        out_specs=(vmem, vmem),
        scratch_shapes=[
            pltpu.VMEM((3, HID, SLICES * 2 * FEAT), BF),
            pltpu.VMEM((2, 3, HPAD, SLICES * LANE), BF),
            pltpu.VMEM((3, 2, HPAD, SLICES * LANE), BF),
            pltpu.VMEM((32, LANE), BF),
            pltpu.VMEM((NZ, 32, LANE), BF),
            pltpu.VMEM((SLICES, LANE, COLS), BF),
            pltpu.VMEM((3, 2 * HPAD, 256), F32),
            pltpu.VMEM((3, 2 * HPAD, 256), F32),
            pltpu.VMEM((4 * HPAD, ROWS), BF),
            pltpu.VMEM((NX - 1, ROWS, WIDE), BF),
            pltpu.VMEM((NX - 1, ROWS, WIDE), BF),
            pltpu.VMEM((NY, ROWS, LANE), BF),
            pltpu.VMEM((NY, ROWS, LANE), BF),
            pltpu.VMEM((NZ, 16, LANE), BF),
            pltpu.VMEM((NZ, 16, LANE), BF),
            dma((3,)),
            dma((1,)),
            dma((2,)),
            dma((2,)),
            dma((NZ,)), dma((NZ,)),
            dma((NX,)), dma((NX,)),
            dma((2, NX, 4)), dma((2, NX, 4)),
            dma((NX,)), dma((NX,)),
            dma((NY,)), dma((NY,)),
            dma((NZ,)), dma((NZ,)),
        ],
        compiler_params=pltpu.CompilerParams(
            collective_id=0, has_side_effects=True, vmem_limit_bytes=48 * 2**20
        ),
    )(tokens, out_grad, expert_ids, gate_probs, w_gate, w_up, w_down)


def solution(mesh):
    in_specs = (
        P("expert", "tensor"),
        P("expert", "tensor"),
        P("expert", None),
        P("expert", None),
        P("expert", "tensor", None),
        P("expert", "tensor", None),
        P("expert", "tensor", None),
    )
    out_specs = (P("expert", "tensor"), P("expert", None))
    return jax.shard_map(body, mesh=mesh, in_specs=in_specs, out_specs=out_specs, check_vma=False)
```

time: 454 us -> 115 us (0.25)
  waiting for transfers between devices: 210 us -> 0 us
  blocking collectives: 159 us -> 0 us
  Pallas kernels: 0 us -> 104 us
  starting transfers between devices: 26 us -> 0 us
  local copies, waits for them, and re-layouts: 33.7 us -> 7.87 us
  between operations: 13.9 us -> 0.64 us
  matrix products: 8.65 us -> 0 us
    all_gather x2 -> x0, waiting for transfers between devices: 154 us -> none  [the longest x1 87.2 us: body(): grad_piece = lax.all_gather(got_grad, 'tensor', axis=1, tiled=True)]
    psum x1 -> x0, blocking collectives: 113 us -> none  [body(): gate_sum = lax.psum(gate_terms, 'tensor')]
    pallas_call x0 -> x1, Pallas kernels: none -> 104 us  [body(): pl.pallas_call(kernel, out_shape=(jax.ShapeDtypeStruct((TOK, FEAT), BF),...]
    all_to_all x2 -> x0, blocking collectives: 46.4 us -> none  [the longest x1 31.2 us: body(): lax.all_to_all(send_rows, 'expert', split_axis=0, concat_axis=0, tiled=True)]
    unnamed x4 -> x0, waiting for transfers between devices: 31.5 us -> none
    all_to_all x2 -> x0, starting transfers between devices: 25.9 us -> none  [the longest x1 13 us: body(): lax.all_to_all(back_gate.astype(jnp.bfloat16), 'expert', split_axis=0, co...]
    all_to_all x2 -> x0, waiting for transfers between devices: 24 us -> none  [the longest x1 12.2 us: body(): lax.all_to_all(back_gate.astype(jnp.bfloat16), 'expert', split_axis=0, co...]
    unnamed x20 -> x13, local copies, waits for them, and re-layouts: 22.6 us -> 7.21 us
  transfers between devices with their start and end apart: 5 -> 0, of which waited for: 5 -> 0; matrix products, arithmetic and copies ran while one was open for 3% -> 0% of each run, Pallas kernels for 0% -> 0%
where the time goes in v1:
time: 115 us; the launch traced here: 112 us
  Pallas kernels  104 us (90%)
  local copies, waits for them, and re-layouts  7.87 us (7%)
    pallas_call x1, Pallas kernels, body(): pl.pallas_call(kernel, out_shape=(jax.ShapeDtypeStruct((TOK, FEAT), BF),...  104 us
    unnamed x13, local copies, waits for them, and re-layouts  7.21 us

profile of v1, /device:TPU:6, one launch (start us, length us, event | category | flops | bytes accessed | tf_op | source)
XLA Modules:
  0.0 112.4 jit_solution(16067810378464977412)
XLA Ops:
  0.6 0.8 copy.9.ids
  1.4 0.8 copy.10.probs
  2.2 0.0 copy-start
  2.2 1.2 %copy-done = bf16[1,84,6144]{2,1,0:T(8,128)(2,1)S(1)} copy-done((bf16[1,84,6144]{2,1,0:T(8,128)(2,1)S(1)}, bf16[1,84,6144]{2,1,0:T(8,128)(2,1)}, u32[]{:S(2)}) %copy-start) | copy-done | bytes 1032216
  3.4 0.0 copy-start.1
  3.4 1.2 %copy-done.1 = bf16[1,84,6144]{2,1,0:T(8,128)(2,1)S(1)} copy-done((bf16[1,84,6144]{2,1,0:T(8,128)(2,1)S(1)}, bf16[1,84,6144]{2,1,0:T(8,128)(2,1)}, u32[]{:S(2)}) %copy-start.1) | copy-done | bytes 1032216
  4.6 0.0 copy-start.2
  4.6 1.2 %copy-done.2 = bf16[1,84,6144]{2,1,0:T(8,128)(2,1)S(1)} copy-done((bf16[1,84,6144]{2,1,0:T(8,128)(2,1)S(1)}, bf16[1,84,6144]{2,1,0:T(8,128)(2,1)}, u32[]{:S(2)}) %copy-start.2) | copy-done | bytes 1032216
  5.9 0.0 copy-start.3
  5.9 0.7 copy-done.3
  6.6 0.0 copy-start.4
  6.6 0.7 copy-done.4
  7.3 103.9 %shard_map.86 = (bf16[12,96]{1,0:T(8,128)(2,1)S(1)}, f32[12,4]{1,0:T(8,128)S(1)}) custom-call(bf16[12,96]{1,0:T(8,128)(2,1)S(1)} %copy-done.3, bf16[12,96]{1,0:T(8,128)(2,1)S(1)} %copy-done.4, s32[12,4]{1,0:T(8,128)S(1)} %copy.9.ids, f32[12,4]{1,0:T(8,128)S(1)} %copy.10.probs, bf16[1,84,6144]{2,1,0:T(8,128)(2,1)S(1)} %copy-done, ...), custom_call_target="tpu_custom_call" | custom-call | tf_op jit(solution)/shard_map/pallas_call | solution.py:313
  111.2 0.7 copy.11
  111.8 0.6 copy.13
Async XLA Ops:
  2.2 1.2 %copy-start = (bf16[1,84,6144]{2,1,0:T(8,128)(2,1)S(1)}, bf16[1,84,6144]{2,1,0:T(8,128)(2,1)}, u32[]{:S(2)}) copy-start(bf16[1,84,6144]{2,1,0:T(8,128)(2,1)} %wg.1) | copy-start | bytes 3096580
  3.4 1.2 %copy-start.1 = (bf16[1,84,6144]{2,1,0:T(8,128)(2,1)S(1)}, bf16[1,84,6144]{2,1,0:T(8,128)(2,1)}, u32[]{:S(2)}) copy-start(bf16[1,84,6144]{2,1,0:T(8,128)(2,1)} %wu.1) | copy-start | bytes 3096580
  4.6 1.2 %copy-start.2 = (bf16[1,84,6144]{2,1,0:T(8,128)(2,1)S(1)}, bf16[1,84,6144]{2,1,0:T(8,128)(2,1)}, u32[]{:S(2)}) copy-start(bf16[1,84,6144]{2,1,0:T(8,128)(2,1)} %wd.1) | copy-start | bytes 3096580
  5.9 0.7 copy-start.3
  6.6 0.7 copy-start.4

commit v2 on v1

v2 whole, which is shorter than its diff:
```python
import jax
import jax.numpy as jnp
from jax import lax
from jax.experimental import pallas as pl
from jax.experimental.pallas import tpu as pltpu
from jax.sharding import PartitionSpec as P

MESH = pl.DeviceIdType.MESH
BF = jnp.bfloat16
F32 = jnp.float32
NZ, NY, NX = 16, 8, 4
SLICES = NY * NX
HID = 84
HPAD = 96
FEAT = 96
LANE = 128
TOK = 12
ROWS = NZ * TOK
COLS = 2 * ROWS
WIDE = NY * LANE


def iota(shape, dim):
    return lax.broadcasted_iota(jnp.int32, shape, dim)


def dot(a, b, ca=1, cb=0):
    return lax.dot_general(a, b, (((ca,), (cb,)), ((), ())), preferred_element_type=F32)


def kernel(
    tok, grad, ids_in, probs_in, wg, wu, wd,
    tg_out, gg_out,
    tin, ids, probs, wraw, wr, wall, zsend, zbuf, xbuf, part, part2, gcat, tmine, tother,
    xs1, xr1, xs2, xr2, ysend, yrecv, rsend, rrecv,
    tsem, wsem, lsem, ssem, csem,
    zss, zrs, xss, xrs, yss, yrs, s1s, s1r, s2s, s2r, rys, ryr, rzs, rzr,
):
    z = lax.axis_index("expert")
    t = lax.axis_index("tensor")
    y = t // 8
    x = lax.rem(t // 2, 4)
    c = lax.rem(t, 2)
    other = 1 - c

    def dev(zz, yy, xx, cc):
        return (zz, (yy * NX + xx) * 2 + cc)

    def zdev(d):
        return dev(lax.rem(z + d, NZ), y, x, c)

    def ydev(d):
        return dev(z, lax.rem(y + d, NY), x, c)

    def xdev(d):
        return dev(z, y, lax.rem(x + d, NX), c)

    sibling = dev(z, y, x, other)

    def remote(src, dst, ss, rs, target):
        return pltpu.make_async_remote_copy(
            src_ref=src, dst_ref=dst, send_sem=ss, recv_sem=rs, device_id=target, device_id_type=MESH
        )

    bar = pltpu.get_barrier_semaphore()

    def greet_z(d, carry):
        pl.semaphore_signal(bar, inc=1, device_id=zdev(d), device_id_type=MESH)
        return carry

    def greet_y(d, carry):
        pl.semaphore_signal(bar, inc=1, device_id=ydev(d), device_id_type=MESH)
        return carry

    def greet_x(d, carry):
        pl.semaphore_signal(bar, inc=1, device_id=xdev(d), device_id_type=MESH)
        return carry

    lax.fori_loop(1, NZ, greet_z, 0)
    lax.fori_loop(1, NY, greet_y, 0)
    lax.fori_loop(1, NX, greet_x, 0)
    pl.semaphore_signal(bar, inc=1, device_id=sibling, device_id_type=MESH)

    heads = [pltpu.make_async_copy(src, tin.at[i], tsem.at[i]) for i, src in enumerate((tok, grad))]
    heads.append(pltpu.make_async_copy(ids_in, ids, tsem.at[2]))
    heads.append(pltpu.make_async_copy(probs_in, probs, tsem.at[3]))
    for cp in heads:
        cp.start()
    loads = [
        pltpu.make_async_copy(src.at[0], wraw.at[i], wsem.at[i]) for i, src in enumerate((wg, wu, wd))
    ]
    for cp in loads:
        cp.start()

    zsend[...] = jnp.zeros_like(zsend)
    for cp in heads:
        cp.wait()
    zsend[0:TOK, 0:FEAT] = tin[0]
    zsend[16:16 + TOK, 0:FEAT] = tin[1]
    zbuf[z] = zsend[...]

    pl.semaphore_wait(bar, (NZ - 1) + (NY - 1) + (NX - 1) + 1)

    def zcopy(d):
        return remote(zsend, zbuf.at[z], zss.at[d], zrs.at[d], zdev(d))

    def zstart(i, carry):
        zcopy(lax.rem(i + 7, 15) + 1).start()
        return carry

    lax.fori_loop(0, NZ - 1, zstart, 0)

    xbuf[:, FEAT:LANE, :] = jnp.zeros((SLICES, LANE - FEAT, COLS), BF)
    wr[:, :, 80:HPAD, :] = jnp.zeros((2, 3, HPAD - 80, SLICES * LANE), BF)
    row = iota((4 * FEAT, 4 * LANE), 0)
    q = (
        (row >= FEAT).astype(jnp.int32)
        + (row >= 2 * FEAT).astype(jnp.int32)
        + (row >= 3 * FEAT).astype(jnp.int32)
    )
    spread = jnp.where(iota((4 * FEAT, 4 * LANE), 1) == row + q * (LANE - FEAT), 1.0, 0.0).astype(BF)
    for cp in loads:
        cp.wait()

    def relay(g, carry):
        yy = g // 2
        xx = 2 * lax.rem(g, 2)
        for i in range(3):
            wide = dot(
                wraw[i, :, pl.ds(pl.multiple_of(g * (4 * FEAT), LANE), 4 * FEAT)], spread
            ).astype(BF)
            for j in range(4):
                at = pl.multiple_of(((xx + j // 2) * NY + yy) * LANE, LANE)
                wr[j % 2, i, 0:HID, pl.ds(at, LANE)] = wide[:, j * LANE:(j + 1) * LANE]
        return carry

    lax.fori_loop(0, 16, relay, 0)
    wsend = remote(wr.at[other], wall.at[:, c], ssem.at[0], ssem.at[1], sibling)
    wsend.start()
    wown = pltpu.make_async_copy(wr.at[c], wall.at[:, c], lsem.at[0])
    wown.start()

    small = iota((TOK, TOK), 0) == iota((TOK, TOK), 1)

    def upright(ref, k, zero):
        return jnp.sum(jnp.where(small, ref[k:k + 1, :], zero), axis=1, keepdims=True)

    chosen = [upright(ids, k, 0) for k in range(4)]
    weight = [upright(probs, k, 0.0) for k in range(4)]

    def zwait(d, carry):
        zcopy(d).wait_recv()
        return carry

    lax.fori_loop(1, NZ, zwait, 0)
    r = iota((NZ * 32, COLS), 0)
    col = iota((NZ * 32, COLS), 1)
    want = ((r >> 4) & 1) * ROWS + (r >> 5) * TOK + (r & 15)
    pick = jnp.where((col == want) & ((r & 15) < TOK), 1.0, 0.0).astype(BF)
    mine = dot(zbuf[...].reshape(NZ * 32, LANE), pick, 0, 0).astype(BF)
    slot = x * NY + y
    xbuf[slot, 0:FEAT, :] = mine[0:FEAT, :]

    def xcopy(d):
        return remote(
            xbuf.at[slot, pl.ds(0, FEAT)], xbuf.at[slot, pl.ds(0, FEAT)], xss.at[d], xrs.at[d], xdev(d)
        )

    for d in (2, 1, 3):
        xcopy(d).start()

    half = FEAT // 2

    def ycopy(i, s, way):
        xx = lax.rem(x + NX - i, NX)
        yy = lax.rem(y + NY - s, NY) if way == 0 else lax.rem(y + s, NY)
        rows = pl.ds(0, FEAT) if s < 3 else pl.ds(way * half, half)
        ref = xbuf.at[xx * NY + yy, rows]
        return remote(ref, ref, yss.at[way, i, s], yrs.at[way, i, s], ydev(1 if way == 0 else NY - 1))

    def forward(i, cores):
        xx = lax.rem(x + NX - i, NX)
        lanes = pl.ds(pl.multiple_of(xx * WIDE, LANE), WIDE)
        blk = xbuf[pl.ds(xx * NY, NY)].reshape(WIDE, COLS)
        for cc in cores:
            pair = wall[0:2, cc, :, lanes].reshape(2 * HPAD, WIDE)
            pair = dot(pair, blk[:, 0:256]).reshape(2, HPAD, 256)
            down = dot(wall[2, cc, :, lanes], blk[:, 128:384])
            if i == 0:
                part[0:2, cc] = pair
                part[2, cc] = down
            else:
                part[0:2, cc] += pair
                part[2, cc] += down

    order = (
        (0, 0), (1, 0), (3, 0), (0, 1), (2, 0), (1, 1), (3, 1), (0, 2),
        (2, 1), (1, 2), (3, 2), (0, 3), (2, 2), (1, 3), (3, 3), (2, 3),
    )
    for i, s in order:
        if s == 0 and i:
            xcopy(i).wait_recv()
        for way in (0, 1):
            if s:
                ycopy(i, s - 1, way).wait_recv()
            ycopy(i, s, way).start()

    wown.wait()
    wsend.wait_recv()
    for i in (0, 1, 3, 2):
        for way in (0, 1):
            ycopy(i, 3, way).wait_recv()
        if i != 2:
            forward(i, (0, 1))
    forward(2, (other,))
    psend = remote(part.at[:, other], part2, csem.at[0], csem.at[1], sibling)
    psend.start()
    forward(2, (c,))
    psend.wait_recv()
    pre_gate = (part[0, c] + part2[0])[:, 0:ROWS]
    pre_up = (part[1, c] + part2[1])[:, 0:ROWS]
    back = (part[2, c] + part2[2])[:, 64:64 + ROWS]
    sig = jax.nn.sigmoid(pre_gate)
    act = pre_gate * sig
    slope = sig * (1.0 + pre_gate * (1.0 - sig))
    hidden = (act * pre_up).astype(BF).astype(F32)
    terms = jnp.sum(hidden * back, axis=0, keepdims=True)
    tmine[:, 0:ROWS] = jnp.broadcast_to(terms, (8, ROWS))
    gcat[0, c, :, 0:ROWS] = (back * pre_up * slope).astype(BF)
    gcat[1, c, :, 0:ROWS] = (back * act).astype(BF)
    tswap = remote(tmine, tother, csem.at[2], csem.at[3], sibling)
    tswap.start()
    gswap = remote(gcat.at[:, c], gcat.at[:, c], csem.at[4], csem.at[5], sibling)
    gswap.start()

    def gate_lanes(column, rows):
        hi = column.astype(BF).astype(F32)
        lane = iota((rows, LANE), 1)
        return jnp.where(lane == FEAT, hi, jnp.where(lane == FEAT + 1, column - hi, 0.0))

    def regate(v, rows):
        lane = iota((rows, LANE), 1)
        gate = jnp.sum(
            jnp.where((lane == FEAT) | (lane == FEAT + 1), v, 0.0), axis=1, keepdims=True
        )
        return gate_lanes(gate, rows), lane < FEAT

    def rewide(v, rows):
        ride, body = regate(v[:, 0:LANE], rows)
        return jnp.where(
            jnp.concatenate([body] * NY, axis=1), v, jnp.concatenate([ride] * NY, axis=1)
        ).astype(BF)

    eye = iota((ROWS, ROWS), 0) == iota((ROWS, ROWS), 1)
    tswap.wait_recv()
    terms = terms + tother[0:1, 0:ROWS]
    column = jnp.sum(jnp.where(eye, terms, 0.0), axis=1, keepdims=True)
    ride = jnp.concatenate([gate_lanes(column, ROWS)] * NY, axis=1)
    gswap.wait_recv()
    gt = gcat[...].reshape(4 * HPAD, 256)[:, 0:ROWS]

    def block(xx):
        lanes = pl.ds(pl.multiple_of(xx * WIDE, LANE), WIDE)
        return dot(gt, wall[0:2, :, :, lanes].reshape(4 * HPAD, WIDE), 0, 0) + ride

    nextx = (xdev(1), xdev(NX - 1))
    part_rows = ROWS // 2
    quarter = part_rows // 2

    def s1copy(h, way):
        return remote(xs1.at[h, way], xr1.at[h, way], s1s.at[h, way], s1r.at[h, way], nextx[way])

    def s2copy(h, way):
        return remote(xs2.at[h, way], xr2.at[h, way], s2s.at[h, way], s2r.at[h, way], nextx[way])

    far = block(lax.rem(x + 2, NX)).astype(BF)
    for h in (0, 1):
        for way in (0, 1):
            at = h * part_rows + way * quarter
            xs1[h, way] = far[at:at + quarter]
            s1copy(h, way).start()
    near = (block(lax.rem(x + 1, NX)), block(lax.rem(x + NX - 1, NX)))
    for h in (0, 1):
        for way in (0, 1):
            for w in (0, 1):
                at = h * part_rows + w * quarter
                mine = near[way][at:at + quarter]
                if w == way:
                    s1copy(h, way).wait_recv()
                    mine = rewide(mine + xr1[h, way].astype(F32), quarter)
                xs2[h, way, w * quarter:(w + 1) * quarter, :] = mine.astype(BF)
            s2copy(h, way).start()
    total = block(x)

    def rycopy(h, d):
        return remote(
            ysend.at[h, lax.rem(y + d, NY)], yrecv.at[h, d], rys.at[h, d], ryr.at[h, d], ydev(d)
        )

    for h in (0, 1):
        v = total[h * part_rows:(h + 1) * part_rows]
        for way in (0, 1):
            s2copy(h, way).wait_recv()
            v = v + xr2[h, way].astype(F32)
        v = rewide(v, part_rows)
        for i in range(NY):
            ysend[h, i] = v[:, i * LANE:(i + 1) * LANE]
        for d in (4, 3, 5, 2, 6, 1, 7):
            rycopy(h, d).start()

    blocks = NZ // 2
    r = iota((blocks * 16, part_rows), 0)
    place = (iota((blocks * 16, part_rows), 1) == (r >> 4) * TOK + (r & 15)) & ((r & 15) < TOK)
    place = jnp.where(place, 1.0, 0.0).astype(BF)

    def rzcopy(d):
        return remote(rsend.at[lax.rem(z + d, NZ)], rrecv.at[z], rzs.at[d], rzr.at[d], zdev(d))

    for h in (0, 1):
        acc = ysend[h, y].astype(F32)
        for d in (1, 7, 2, 6, 3, 5, 4):
            rycopy(h, d).wait_recv()
            acc = acc + yrecv[h, d].astype(F32)
        ride, body = regate(acc, part_rows)
        acc = jnp.where(body, acc, ride).astype(BF)
        rsend[h * blocks:(h + 1) * blocks] = dot(place, acc).astype(BF).reshape(blocks, 16, LANE)

        def rzstart(j, carry):
            target = h * blocks + j

            @pl.when(target != z)
            def _():
                rzcopy(lax.rem(target + NZ - z, NZ)).start()

            return carry

        lax.fori_loop(0, blocks, rzstart, 0)
    rrecv[z] = rsend[z]

    def rzwait(d, carry):
        rzcopy(d).wait_recv()
        return carry

    lax.fori_loop(1, NZ, rzwait, 0)
    out = jnp.zeros((TOK, LANE), F32)
    gout = [jnp.zeros((TOK, 1), F32) for _ in range(4)]
    for e in range(NZ // 2):
        hits = [chosen[k] == e for k in range(4)]
        w = jnp.zeros((TOK, 1), F32)
        for k in range(4):
            w = w + jnp.where(hits[k], weight[k], 0.0)
        v = rrecv[2 * e].astype(F32) + rrecv[2 * e + 1].astype(F32)
        v = v[0:TOK]
        out = out + w * v
        gate = v[:, FEAT:FEAT + 1] + v[:, FEAT + 1:FEAT + 2]
        gout = [gout[k] + jnp.where(hits[k], gate, 0.0) for k in range(4)]
    tg_out[...] = out[:, 0:FEAT].astype(BF)
    for k in range(4):
        gg_out[k:k + 1, :] = jnp.sum(jnp.where(small, gout[k], 0.0), axis=0, keepdims=True)

    def zdone(d, carry):
        zcopy(d).wait_send()
        rzcopy(d).wait_send()
        return carry

    lax.fori_loop(1, NZ, zdone, 0)
    wsend.wait_send()
    for cp in (psend, tswap, gswap):
        cp.wait_send()
    for d in range(1, NX):
        xcopy(d).wait_send()
    for h in (0, 1):
        for way in (0, 1):
            s1copy(h, way).wait_send()
            s2copy(h, way).wait_send()
        for d in range(1, NY):
            rycopy(h, d).wait_send()
    for s in range(4):
        for i in range(NX):
            for way in (0, 1):
                ycopy(i, s, way).wait_send()


def body(tokens, out_grad, expert_ids, gate_probs, w_gate, w_up, w_down):
    vmem = pl.BlockSpec(memory_space=pltpu.VMEM)
    hbm = pl.BlockSpec(memory_space=pltpu.HBM)
    dma = pltpu.SemaphoreType.DMA
    token_grad, gate_grad = pl.pallas_call(
        kernel,
        out_shape=(
            jax.ShapeDtypeStruct((TOK, FEAT), BF),
            jax.ShapeDtypeStruct((4, TOK), F32),
        ),
        in_specs=[hbm] * 7,
        out_specs=(vmem, vmem),
        scratch_shapes=[
            pltpu.VMEM((2, TOK, FEAT), BF),
            pltpu.VMEM((4, TOK), jnp.int32),
            pltpu.VMEM((4, TOK), F32),
            pltpu.VMEM((3, HID, SLICES * 2 * FEAT), BF),
            pltpu.VMEM((2, 3, HPAD, SLICES * LANE), BF),
            pltpu.VMEM((3, 2, HPAD, SLICES * LANE), BF),
            pltpu.VMEM((32, LANE), BF),
            pltpu.VMEM((NZ, 32, LANE), BF),
            pltpu.VMEM((SLICES, LANE, COLS), BF),
            pltpu.VMEM((3, 2, HPAD, 256), F32),
            pltpu.VMEM((3, HPAD, 256), F32),
            pltpu.VMEM((2, 2, HPAD, 256), BF),
            pltpu.VMEM((8, 256), F32),
            pltpu.VMEM((8, 256), F32),
            pltpu.VMEM((2, 2, ROWS // 4, WIDE), BF),
            pltpu.VMEM((2, 2, ROWS // 4, WIDE), BF),
            pltpu.VMEM((2, 2, ROWS // 2, WIDE), BF),
            pltpu.VMEM((2, 2, ROWS // 2, WIDE), BF),
            pltpu.VMEM((2, NY, ROWS // 2, LANE), BF),
            pltpu.VMEM((2, NY, ROWS // 2, LANE), BF),
            pltpu.VMEM((NZ, 16, LANE), BF),
            pltpu.VMEM((NZ, 16, LANE), BF),
            dma((4,)),
            dma((3,)),
            dma((1,)),
            dma((2,)),
            dma((6,)),
            dma((NZ,)), dma((NZ,)),
            dma((NX,)), dma((NX,)),
            dma((2, NX, 4)), dma((2, NX, 4)),
            dma((2, 2)), dma((2, 2)),
            dma((2, 2)), dma((2, 2)),
            dma((2, NY)), dma((2, NY)),
            dma((NZ,)), dma((NZ,)),
        ],
        compiler_params=pltpu.CompilerParams(
            collective_id=0, has_side_effects=True, vmem_limit_bytes=63 * 2**20
        ),
    )(tokens, out_grad, expert_ids.T, gate_probs.T, w_gate, w_up, w_down)
    return token_grad, gate_grad.T


def solution(mesh):
    in_specs = (
        P("expert", "tensor"),
        P("expert", "tensor"),
        P("expert", None),
        P("expert", None),
        P("expert", "tensor", None),
        P("expert", "tensor", None),
        P("expert", "tensor", None),
    )
    out_specs = (P("expert", "tensor"), P("expert", None))
    return jax.shard_map(body, mesh=mesh, in_specs=in_specs, out_specs=out_specs, check_vma=False)
```

time: 115 us -> 96.1 us (0.84); the launches traced: 112 us -> 95.9 us
  Pallas kernels: 104 us -> 92.8 us
  local copies, waits for them, and re-layouts: 7.87 us -> 2.5 us
    pallas_call x1, Pallas kernels: 104 us -> 92.8 us  [body(): pl.pallas_call(kernel, out_shape=(jax.ShapeDtypeStruct((TOK, FEAT), BF),...]
    unnamed x13 -> x2, local copies, waits for them, and re-layouts: 7.21 us -> 2.5 us
where the time goes in v2:
time: 96.1 us; the launch traced here: 95.9 us
  Pallas kernels  92.8 us (97%)
  local copies, waits for them, and re-layouts  2.5 us (3%)
    pallas_call x1, Pallas kernels, body(): pl.pallas_call(kernel, out_shape=(jax.ShapeDtypeStruct((TOK, FEAT), BF),...  92.8 us
    unnamed x2, local copies, waits for them, and re-layouts  2.5 us

profile of v2, /device:TPU:6, one launch (start us, length us, event | category | flops | bytes accessed | tf_op | source)
XLA Modules:
  0.0 95.9 jit_solution(1816989504165671261)
XLA Ops:
  0.6 92.8 %shard_map.86 = (bf16[12,96]{1,0:T(8,128)(2,1)}, f32[4,12]{1,0:T(4,128)}) custom-call(bf16[12,96]{1,0:T(8,128)(2,1)} %tok.1, bf16[12,96]{1,0:T(8,128)(2,1)} %grad.1, s32[4,12]{1,0:T(4,128)} %bitcast.3, f32[4,12]{1,0:T(4,128)} %bitcast.4, bf16[1,84,6144]{2,1,0:T(8,128)(2,1)} %wg.1, bf16[1,84,6144]{2,1,0:T(8,128)(2,1)} %wu.1, bf16[1,84,6144]{2,1,0:T(8,128)(2,1)} %wd.1), custom_call_target="tpu_custom_call" | custom-call | tf_op jit(solution)/shard_map/pallas_call | solution.py:388
  93.4 1.3 %copy.11 = bf16[12,96]{1,0:T(8,128)(2,1)} copy(bf16[12,96]{1,0:T(8,128)(2,1)} %get-tuple-element.8) | data formatting | bytes 4608
  94.7 1.2 %copy.12 = f32[12,4]{0,1:T(4,128)} copy(f32[12,4]{0,1:T(4,128)} %bitcast.5) | data formatting | bytes 384

commit v3 on v2

v3 whole, which is shorter than its diff:
```python
import jax
import jax.numpy as jnp
from jax import lax
from jax.experimental import pallas as pl
from jax.experimental.pallas import tpu as pltpu
from jax.sharding import PartitionSpec as P

MESH = pl.DeviceIdType.MESH
BF = jnp.bfloat16
F32 = jnp.float32
NZ, NY, NX = 16, 8, 4
SLICES = NY * NX
HID = 84
HPAD = 96
FEAT = 96
LANE = 128
TOK = 12
ROWS = NZ * TOK
WIDE = NX * LANE


def iota(shape, dim):
    return lax.broadcasted_iota(jnp.int32, shape, dim)


def dot(a, b, ca=1, cb=0):
    return lax.dot_general(a, b, (((ca,), (cb,)), ((), ())), preferred_element_type=F32)


def kernel(
    tok, grad, ids_in, probs_in, wg, wu, wd,
    tg_out, gg_out,
    tin, ids, probs, wraw, wr, wall, zsend, zbuf, xnear, xrest, part, part2, gcat, tmine, tother,
    bwd, xs1, xr1, xs2, xr2, ysend, yrecv, rsend, rrecv,
    tsem, wsem, lsem, ssem, csem,
    zss, zrs, yss, yrs, x1s, x1r, x2s, x2r, s1s, s1r, s2s, s2r, rys, ryr, rzs, rzr,
):
    z = lax.axis_index("expert")
    t = lax.axis_index("tensor")
    y = t // 8
    x = lax.rem(t // 2, 4)
    c = lax.rem(t, 2)
    other = 1 - c

    def dev(zz, yy, xx, cc):
        return (zz, (yy * NX + xx) * 2 + cc)

    def zdev(d):
        return dev(lax.rem(z + d, NZ), y, x, c)

    def ydev(d):
        return dev(z, lax.rem(y + d, NY), x, c)

    def xdev(d):
        return dev(z, y, lax.rem(x + d, NX), c)

    sibling = dev(z, y, x, other)

    def remote(src, dst, ss, rs, target):
        return pltpu.make_async_remote_copy(
            src_ref=src, dst_ref=dst, send_sem=ss, recv_sem=rs, device_id=target, device_id_type=MESH
        )

    bar = pltpu.get_barrier_semaphore()

    def greet_z(d, carry):
        pl.semaphore_signal(bar, inc=1, device_id=zdev(d), device_id_type=MESH)
        return carry

    def greet_y(d, carry):
        pl.semaphore_signal(bar, inc=1, device_id=ydev(d), device_id_type=MESH)
        return carry

    def greet_x(d, carry):
        pl.semaphore_signal(bar, inc=1, device_id=xdev(d), device_id_type=MESH)
        return carry

    lax.fori_loop(1, NZ, greet_z, 0)
    lax.fori_loop(1, NY, greet_y, 0)
    lax.fori_loop(1, NX, greet_x, 0)
    pl.semaphore_signal(bar, inc=1, device_id=sibling, device_id_type=MESH)

    heads = [pltpu.make_async_copy(src, tin.at[i], tsem.at[i]) for i, src in enumerate((tok, grad))]
    heads.append(pltpu.make_async_copy(ids_in, ids, tsem.at[2]))
    heads.append(pltpu.make_async_copy(probs_in, probs, tsem.at[3]))
    for cp in heads:
        cp.start()
    loads = [
        pltpu.make_async_copy(src.at[0], wraw.at[i], wsem.at[i]) for i, src in enumerate((wg, wu, wd))
    ]
    for cp in loads:
        cp.start()

    zsend[...] = jnp.zeros_like(zsend)
    for cp in heads:
        cp.wait()
    zsend[0:TOK, 0:FEAT] = tin[0]
    zsend[16:16 + TOK, 0:FEAT] = tin[1]
    zbuf[0] = zsend[...]

    pl.semaphore_wait(bar, (NZ - 1) + (NY - 1) + (NX - 1) + 1)

    def place_of(d):
        return 2 * d - 1 if 0 < d < 8 else (2 * (NZ - d) if d > 8 else (15 if d else 0))

    z_order = (1, 15, 2, 14, 3, 13, 4, 12, 5, 11, 6, 10, 7, 9, 8)

    def zcopy(d):
        return remote(zsend, zbuf.at[place_of(NZ - d)], zss.at[d], zrs.at[d], zdev(d))

    for d in z_order:
        zcopy(d).start()

    xnear[:, FEAT:LANE, :] = jnp.zeros((SLICES, LANE - FEAT, LANE), BF)
    xrest[:, FEAT:LANE, :] = jnp.zeros((SLICES, LANE - FEAT, 2 * LANE), BF)
    wr[:, :, 80:HPAD, :] = jnp.zeros((2, 3, HPAD - 80, SLICES * LANE), BF)
    row = iota((4 * FEAT, 4 * LANE), 0)
    q = (
        (row >= FEAT).astype(jnp.int32)
        + (row >= 2 * FEAT).astype(jnp.int32)
        + (row >= 3 * FEAT).astype(jnp.int32)
    )
    spread = jnp.where(iota((4 * FEAT, 4 * LANE), 1) == row + q * (LANE - FEAT), 1.0, 0.0).astype(BF)
    for cp in loads:
        cp.wait()

    def relay(g, carry):
        yy = g // 2
        xx = 2 * lax.rem(g, 2)
        for i in range(3):
            wide = dot(
                wraw[i, :, pl.ds(pl.multiple_of(g * (4 * FEAT), LANE), 4 * FEAT)], spread
            ).astype(BF)
            for j in range(4):
                at = pl.multiple_of((yy * NX + xx + j // 2) * LANE, LANE)
                wr[j % 2, i, 0:HID, pl.ds(at, LANE)] = wide[:, j * LANE:(j + 1) * LANE]
        return carry

    lax.fori_loop(0, 16, relay, 0)
    wsend = remote(wr.at[other], wall.at[:, c], ssem.at[0], ssem.at[1], sibling)
    wsend.start()
    wown = pltpu.make_async_copy(wr.at[c], wall.at[:, c], lsem.at[0])
    wown.start()

    small = iota((TOK, TOK), 0) == iota((TOK, TOK), 1)

    def upright(ref, k, zero):
        return jnp.sum(jnp.where(small, ref[k:k + 1, :], zero), axis=1, keepdims=True)

    chosen = [upright(ids, k, 0) for k in range(4)]
    weight = [upright(probs, k, 0.0) for k in range(4)]

    slot = y * NX + x
    bufs = (xnear, xrest)
    counts = (64, ROWS - 64)
    spans = ((0, 6), (5, NZ))

    def turn(g):
        first, end = spans[g]
        shape = ((end - first) * 32, 2 * counts[g])
        r = iota(shape, 0)
        p = ((r >> 5) + first) * TOK + (r & 15) - 64 * g
        col = ((r >> 4) & 1) * counts[g] + p
        fit = (p >= 0) & (p < counts[g]) & ((r & 15) < TOK) & (iota(shape, 1) == col)
        rows = zbuf[first:end].reshape(shape[0], LANE)
        mine = dot(rows, jnp.where(fit, 1.0, 0.0).astype(BF), 0, 0).astype(BF)
        bufs[g][slot, 0:FEAT, :] = mine[0:FEAT, :]

    half = FEAT // 2
    nextx = (xdev(1), xdev(NX - 1))
    near_first = (1, 7, 2, 6, 3, 5, 4)
    blocks_in = (0,) + near_first

    def ycopy(g, d):
        ref = bufs[g].at[slot, pl.ds(0, FEAT)]
        return remote(ref, ref, yss.at[g, d], yrs.at[g, d], ydev(d))

    def x1copy(g, d, way):
        ref = bufs[g].at[lax.rem(y + NY - d, NY) * NX + x, pl.ds(0, FEAT)]
        return remote(ref, ref, x1s.at[g, d, way], x1r.at[g, d, way], nextx[way])

    def x2copy(g, d, way):
        xx = lax.rem(x + (NX - 1 if way == 0 else 1), NX)
        ref = bufs[g].at[lax.rem(y + NY - d, NY) * NX + xx, pl.ds(way * half, half)]
        return remote(ref, ref, x2s.at[g, d, way], x2r.at[g, d, way], nextx[way])

    def launch(g):
        turn(g)
        for way in (0, 1):
            x1copy(g, 0, way).start()
        for d in near_first:
            ycopy(g, d).start()

    def across(g, ds):
        for d in ds:
            ycopy(g, d).wait_recv()
            for way in (0, 1):
                x1copy(g, d, way).start()

    def onward(g):
        for d in blocks_in:
            for way in (0, 1):
                x1copy(g, d, way).wait_recv()
                x2copy(g, d, way).start()

    early = (15, 1, 14, 2, 13)
    for d in early:
        zcopy(d).wait_recv()
    launch(0)
    across(0, near_first[:4])
    for d in z_order:
        if d not in early:
            zcopy(d).wait_recv()
    launch(1)
    across(0, near_first[4:])
    onward(0)
    across(1, near_first)
    onward(1)

    def forward(d, cores):
        yy = lax.rem(y + NY - d, NY)
        lanes = pl.ds(pl.multiple_of(yy * WIDE, LANE), WIDE)
        near = xnear[pl.ds(yy * NX, NX)].reshape(WIDE, LANE)
        rest = xrest[pl.ds(yy * NX, NX)].reshape(WIDE, 2 * LANE)
        toks = jnp.concatenate([near, rest[:, 0:LANE]], axis=1)
        grads = jnp.concatenate([near, rest[:, LANE:2 * LANE]], axis=1)
        for cc in cores:
            pair = wall[0:2, cc, :, lanes].reshape(2 * HPAD, WIDE)
            pair = dot(pair, toks).reshape(2, HPAD, 256)
            down = dot(wall[2, cc, :, lanes], grads)
            if d == 0:
                part[0:2, cc] = pair
                part[2, cc] = down
            else:
                part[0:2, cc] += pair
                part[2, cc] += down

    wown.wait()
    wsend.wait_recv()
    for d in blocks_in:
        for g in (0, 1):
            for way in (0, 1):
                x2copy(g, d, way).wait_recv()
        if d != 4:
            forward(d, (0, 1))
    forward(4, (other,))
    psend = remote(part.at[:, other], part2, csem.at[0], csem.at[1], sibling)
    psend.start()
    forward(4, (c,))
    psend.wait_recv()

    def tokens_of(v):
        return jnp.concatenate([v[:, 0:64], v[:, LANE:2 * LANE]], axis=1)

    pre_gate = tokens_of(part[0, c] + part2[0])
    pre_up = tokens_of(part[1, c] + part2[1])
    back = (part[2, c] + part2[2])[:, 64:64 + ROWS]
    sig = jax.nn.sigmoid(pre_gate)
    act = pre_gate * sig
    slope = sig * (1.0 + pre_gate * (1.0 - sig))
    hidden = (act * pre_up).astype(BF).astype(F32)
    terms = jnp.sum(hidden * back, axis=0, keepdims=True)
    tmine[:, 0:ROWS] = jnp.broadcast_to(terms, (8, ROWS))
    gcat[0, c, :, 0:ROWS] = (back * pre_up * slope).astype(BF)
    gcat[1, c, :, 0:ROWS] = (back * act).astype(BF)
    tswap = remote(tmine, tother, csem.at[2], csem.at[3], sibling)
    tswap.start()
    gswap = remote(gcat.at[:, c], gcat.at[:, c], csem.at[4], csem.at[5], sibling)
    gswap.start()

    def gate_lanes(column, rows):
        hi = column.astype(BF).astype(F32)
        lane = iota((rows, LANE), 1)
        return jnp.where(lane == FEAT, hi, jnp.where(lane == FEAT + 1, column - hi, 0.0))

    def regate(v, rows):
        lane = iota((rows, LANE), 1)
        gate = jnp.sum(
            jnp.where((lane == FEAT) | (lane == FEAT + 1), v, 0.0), axis=1, keepdims=True
        )
        return gate_lanes(gate, rows), lane < FEAT

    def sealed(v, rows):
        ride, body = regate(v, rows)
        return jnp.where(body, v, ride).astype(BF)

    eye = iota((ROWS, ROWS), 0) == iota((ROWS, ROWS), 1)
    tswap.wait_recv()
    terms = terms + tother[0:1, 0:ROWS]
    column = jnp.sum(jnp.where(eye, terms, 0.0), axis=1, keepdims=True)
    ride = jnp.concatenate([gate_lanes(column, ROWS)] * NX, axis=1)
    gswap.wait_recv()
    gt = gcat[...].reshape(4 * HPAD, 256)[:, 0:ROWS]

    far_first = (4, 3, 5, 2, 6, 1, 7, 0)
    part_rows = ROWS // 2

    def s1copy(d, way):
        return remote(xs1.at[d, way], xr1.at[d, way], s1s.at[d, way], s1r.at[d, way], nextx[way])

    def s2copy(d, way):
        return remote(xs2.at[d, way], xr2.at[d, way], s2s.at[d, way], s2r.at[d, way], nextx[way])

    def xlanes(k):
        return pl.ds(pl.multiple_of(lax.rem(x + k, NX) * LANE, LANE), LANE)

    for d in far_first:
        lanes = pl.ds(pl.multiple_of(lax.rem(y + d, NY) * WIDE, LANE), WIDE)
        bwd[d] = dot(gt, wall[0:2, :, :, lanes].reshape(4 * HPAD, WIDE), 0, 0) + ride
        for way in (0, 1):
            rows = pl.ds(way * part_rows, part_rows)
            xs1[d, way] = bwd[d, rows, xlanes(2)].astype(BF)
            s1copy(d, way).start()
    for d in far_first:
        for way in (0, 1):
            near = xlanes(1 if way == 0 else NX - 1)
            rest = pl.ds((1 - way) * part_rows, part_rows)
            xs2[d, way, rest, :] = bwd[d, rest, near].astype(BF)
            rows = pl.ds(way * part_rows, part_rows)
            s1copy(d, way).wait_recv()
            mine = bwd[d, rows, near] + xr1[d, way].astype(F32)
            xs2[d, way, rows, :] = sealed(mine, part_rows)
            s2copy(d, way).start()

    def rycopy(d):
        return remote(ysend.at[d], yrecv.at[d], rys.at[d], ryr.at[d], ydev(d))

    for d in far_first:
        v = bwd[d, :, xlanes(0)]
        for way in (0, 1):
            s2copy(d, way).wait_recv()
            v = v + xr2[d, way].astype(F32)
        if d:
            ysend[d] = sealed(v, ROWS)
            rycopy(d).start()
        else:
            acc = v

    for d in far_first[:NY - 1]:
        rycopy(d).wait_recv()
        acc = acc + yrecv[d].astype(F32)
    r = iota((NZ * 16, ROWS), 0)
    place = (iota((NZ * 16, ROWS), 1) == (r >> 4) * TOK + (r & 15)) & ((r & 15) < TOK)
    place = jnp.where(place, 1.0, 0.0).astype(BF)
    rsend[...] = dot(place, sealed(acc, ROWS)).astype(BF).reshape(NZ, 16, LANE)
    rrecv[z] = rsend[0]

    def rzcopy(d):
        return remote(rsend.at[place_of(d)], rrecv.at[z], rzs.at[d], rzr.at[d], zdev(d))

    for d in z_order[::-1]:
        rzcopy(d).start()

    for d in z_order:
        rzcopy(d).wait_recv()
    out = jnp.zeros((TOK, LANE), F32)
    gout = [jnp.zeros((TOK, 1), F32) for _ in range(4)]
    for e in range(NZ // 2):
        hits = [chosen[k] == e for k in range(4)]
        w = jnp.zeros((TOK, 1), F32)
        for k in range(4):
            w = w + jnp.where(hits[k], weight[k], 0.0)
        v = rrecv[2 * e].astype(F32) + rrecv[2 * e + 1].astype(F32)
        v = v[0:TOK]
        out = out + w * v
        gate = v[:, FEAT:FEAT + 1] + v[:, FEAT + 1:FEAT + 2]
        gout = [gout[k] + jnp.where(hits[k], gate, 0.0) for k in range(4)]
    tg_out[...] = out[:, 0:FEAT].astype(BF)
    for k in range(4):
        gg_out[k:k + 1, :] = jnp.sum(jnp.where(small, gout[k], 0.0), axis=0, keepdims=True)

    for d in z_order:
        zcopy(d).wait_send()
        rzcopy(d).wait_send()
    wsend.wait_send()
    for cp in (psend, tswap, gswap):
        cp.wait_send()
    for d in range(NY):
        if d:
            rycopy(d).wait_send()
            for g in (0, 1):
                ycopy(g, d).wait_send()
        for way in (0, 1):
            for g in (0, 1):
                x1copy(g, d, way).wait_send()
                x2copy(g, d, way).wait_send()
            s1copy(d, way).wait_send()
            s2copy(d, way).wait_send()


def body(tokens, out_grad, expert_ids, gate_probs, w_gate, w_up, w_down):
    vmem = pl.BlockSpec(memory_space=pltpu.VMEM)
    hbm = pl.BlockSpec(memory_space=pltpu.HBM)
    dma = pltpu.SemaphoreType.DMA
    token_grad, gate_grad = pl.pallas_call(
        kernel,
        out_shape=(
            jax.ShapeDtypeStruct((TOK, FEAT), BF),
            jax.ShapeDtypeStruct((4, TOK), F32),
        ),
        in_specs=[hbm] * 7,
        out_specs=(vmem, vmem),
        scratch_shapes=[
            pltpu.VMEM((2, TOK, FEAT), BF),
            pltpu.VMEM((4, TOK), jnp.int32),
            pltpu.VMEM((4, TOK), F32),
            pltpu.VMEM((3, HID, SLICES * 2 * FEAT), BF),
            pltpu.VMEM((2, 3, HPAD, SLICES * LANE), BF),
            pltpu.VMEM((3, 2, HPAD, SLICES * LANE), BF),
            pltpu.VMEM((32, LANE), BF),
            pltpu.VMEM((NZ, 32, LANE), BF),
            pltpu.VMEM((SLICES, LANE, LANE), BF),
            pltpu.VMEM((SLICES, LANE, 2 * LANE), BF),
            pltpu.VMEM((3, 2, HPAD, 256), F32),
            pltpu.VMEM((3, HPAD, 256), F32),
            pltpu.VMEM((2, 2, HPAD, 256), BF),
            pltpu.VMEM((8, 256), F32),
            pltpu.VMEM((8, 256), F32),
            pltpu.VMEM((NY, ROWS, WIDE), F32),
            pltpu.VMEM((NY, 2, ROWS // 2, LANE), BF),
            pltpu.VMEM((NY, 2, ROWS // 2, LANE), BF),
            pltpu.VMEM((NY, 2, ROWS, LANE), BF),
            pltpu.VMEM((NY, 2, ROWS, LANE), BF),
            pltpu.VMEM((NY, ROWS, LANE), BF),
            pltpu.VMEM((NY, ROWS, LANE), BF),
            pltpu.VMEM((NZ, 16, LANE), BF),
            pltpu.VMEM((NZ, 16, LANE), BF),
            dma((4,)),
            dma((3,)),
            dma((1,)),
            dma((2,)),
            dma((6,)),
            dma((NZ,)), dma((NZ,)),
            dma((2, NY)), dma((2, NY)),
            dma((2, NY, 2)), dma((2, NY, 2)),
            dma((2, NY, 2)), dma((2, NY, 2)),
            dma((NY, 2)), dma((NY, 2)),
            dma((NY, 2)), dma((NY, 2)),
            dma((NY,)), dma((NY,)),
            dma((NZ,)), dma((NZ,)),
        ],
        compiler_params=pltpu.CompilerParams(
            collective_id=0, has_side_effects=True, vmem_limit_bytes=63 * 2**20
        ),
    )(tokens, out_grad, expert_ids.T, gate_probs.T, w_gate, w_up, w_down)
    return token_grad, gate_grad.T


def solution(mesh):
    in_specs = (
        P("expert", "tensor"),
        P("expert", "tensor"),
        P("expert", None),
        P("expert", None),
        P("expert", "tensor", None),
        P("expert", "tensor", None),
        P("expert", "tensor", None),
    )
    out_specs = (P("expert", "tensor"), P("expert", None))
    return jax.shard_map(body, mesh=mesh, in_specs=in_specs, out_specs=out_specs, check_vma=False)
```

time: 96.1 us -> 89.2 us (0.928); the launches traced: 95.9 us -> 87.5 us
  Pallas kernels: 92.8 us -> 84.4 us
    pallas_call x1, Pallas kernels: 92.8 us -> 84.4 us  [body(): pl.pallas_call(kernel, out_shape=(jax.ShapeDtypeStruct((TOK, FEAT), BF),...]
where the time goes in v3:
time: 89.2 us; the launch traced here: 87.5 us
  Pallas kernels  84.4 us (95%)
  local copies, waits for them, and re-layouts  2.5 us (3%)
    pallas_call x1, Pallas kernels, body(): pl.pallas_call(kernel, out_shape=(jax.ShapeDtypeStruct((TOK, FEAT), BF),...  84.4 us
    unnamed x2, local copies, waits for them, and re-layouts  2.5 us

profile of v3, /device:TPU:6, one launch (start us, length us, event | category | flops | bytes accessed | tf_op | source)
XLA Modules:
  0.0 87.5 jit_solution(1393329250958912564)
XLA Ops:
  0.6 84.4 %shard_map.86 = (bf16[12,96]{1,0:T(8,128)(2,1)}, f32[4,12]{1,0:T(4,128)}) custom-call(bf16[12,96]{1,0:T(8,128)(2,1)} %tok.1, bf16[12,96]{1,0:T(8,128)(2,1)} %grad.1, s32[4,12]{1,0:T(4,128)} %bitcast.3, f32[4,12]{1,0:T(4,128)} %bitcast.4, bf16[1,84,6144]{2,1,0:T(8,128)(2,1)} %wg.1, bf16[1,84,6144]{2,1,0:T(8,128)(2,1)} %wu.1, bf16[1,84,6144]{2,1,0:T(8,128)(2,1)} %wd.1), custom_call_target="tpu_custom_call" | custom-call | tf_op jit(solution)/shard_map/pallas_call | solution.py:395
  85.0 1.3 %copy.11 = bf16[12,96]{1,0:T(8,128)(2,1)} copy(bf16[12,96]{1,0:T(8,128)(2,1)} %get-tuple-element.8) | data formatting | bytes 4608
  86.3 1.2 %copy.12 = f32[12,4]{0,1:T(4,128)} copy(f32[12,4]{0,1:T(4,128)} %bitcast.5) | data formatting | bytes 384

commit v4 on v3

--- a/solution.py
+++ b/solution.py
@@ -293,63 +293,91 @@
     gt = gcat[...].reshape(4 * HPAD, 256)[:, 0:ROWS]
 
     far_first = (4, 3, 5, 2, 6, 1, 7, 0)
-    part_rows = ROWS // 2
-
-    def s1copy(d, way):
-        return remote(xs1.at[d, way], xr1.at[d, way], s1s.at[d, way], s1r.at[d, way], nextx[way])
-
-    def s2copy(d, way):
-        return remote(xs2.at[d, way], xr2.at[d, way], s2s.at[d, way], s2r.at[d, way], nextx[way])
+    bases = (0, 64)
+
+    def s1copy(g, d, way):
+        at = pl.ds(bases[g] // 2, counts[g] // 2)
+        return remote(
+            xs1.at[d, way, at], xr1.at[d, way, at], s1s.at[g, d, way], s1r.at[g, d, way], nextx[way]
+        )
+
+    def s2copy(g, d, way):
+        at = pl.ds(bases[g], counts[g])
+        return remote(
+            xs2.at[d, way, at], xr2.at[d, way, at], s2s.at[g, d, way], s2r.at[g, d, way], nextx[way]
+        )
 
     def xlanes(k):
         return pl.ds(pl.multiple_of(lax.rem(x + k, NX) * LANE, LANE), LANE)
+
+    def first_step(g, d):
+        n = counts[g] // 2
+        for way in (0, 1):
+            rows = pl.ds(bases[g] + way * n, n)
+            xs1[d, way, pl.ds(bases[g] // 2, n), :] = bwd[d, rows, xlanes(2)].astype(BF)
+            s1copy(g, d, way).start()
 
     for d in far_first:
         lanes = pl.ds(pl.multiple_of(lax.rem(y + d, NY) * WIDE, LANE), WIDE)
         bwd[d] = dot(gt, wall[0:2, :, :, lanes].reshape(4 * HPAD, WIDE), 0, 0) + ride
-        for way in (0, 1):
-            rows = pl.ds(way * part_rows, part_rows)
-            xs1[d, way] = bwd[d, rows, xlanes(2)].astype(BF)
-            s1copy(d, way).start()
+        first_step(1, d)
     for d in far_first:
-        for way in (0, 1):
-            near = xlanes(1 if way == 0 else NX - 1)
-            rest = pl.ds((1 - way) * part_rows, part_rows)
-            xs2[d, way, rest, :] = bwd[d, rest, near].astype(BF)
-            rows = pl.ds(way * part_rows, part_rows)
-            s1copy(d, way).wait_recv()
-            mine = bwd[d, rows, near] + xr1[d, way].astype(F32)
-            xs2[d, way, rows, :] = sealed(mine, part_rows)
-            s2copy(d, way).start()
-
-    def rycopy(d):
-        return remote(ysend.at[d], yrecv.at[d], rys.at[d], ryr.at[d], ydev(d))
-
-    for d in far_first:
-        v = bwd[d, :, xlanes(0)]
-        for way in (0, 1):
-            s2copy(d, way).wait_recv()
-            v = v + xr2[d, way].astype(F32)
-        if d:
-            ysend[d] = sealed(v, ROWS)
-            rycopy(d).start()
-        else:
-            acc = v
-
-    for d in far_first[:NY - 1]:
-        rycopy(d).wait_recv()
-        acc = acc + yrecv[d].astype(F32)
-    r = iota((NZ * 16, ROWS), 0)
-    place = (iota((NZ * 16, ROWS), 1) == (r >> 4) * TOK + (r & 15)) & ((r & 15) < TOK)
-    place = jnp.where(place, 1.0, 0.0).astype(BF)
-    rsend[...] = dot(place, sealed(acc, ROWS)).astype(BF).reshape(NZ, 16, LANE)
-    rrecv[z] = rsend[0]
+        first_step(0, d)
+    for g in (1, 0):
+        n = counts[g] // 2
+        for d in far_first:
+            for way in (0, 1):
+                near = xlanes(1 if way == 0 else NX - 1)
+                rest = pl.ds(bases[g] + (1 - way) * n, n)
+                xs2[d, way, rest, :] = bwd[d, rest, near].astype(BF)
+                rows = pl.ds(bases[g] + way * n, n)
+                s1copy(g, d, way).wait_recv()
+                mine = bwd[d, rows, near] + xr1[d, way, pl.ds(bases[g] // 2, n), :].astype(F32)
+                xs2[d, way, rows, :] = sealed(mine, n)
+                s2copy(g, d, way).start()
+
+    def rycopy(g, d):
+        at = pl.ds(bases[g], counts[g])
+        return remote(ysend.at[d, at], yrecv.at[d, at], rys.at[g, d], ryr.at[g, d], ydev(d))
+
+    accs = [None, None]
+    for g in (1, 0):
+        at = pl.ds(bases[g], counts[g])
+        for d in far_first:
+            v = bwd[d, at, xlanes(0)]
+            for way in (0, 1):
+                s2copy(g, d, way).wait_recv()
+                v = v + xr2[d, way, at, :].astype(F32)
+            if d:
+                ysend[d, at, :] = sealed(v, counts[g])
+                rycopy(g, d).start()
+            else:
+                accs[g] = v
 
     def rzcopy(d):
         return remote(rsend.at[place_of(d)], rrecv.at[z], rzs.at[d], rzr.at[d], zdev(d))
 
-    for d in z_order[::-1]:
-        rzcopy(d).start()
+    def send_back(v, base, first, end):
+        shape = ((end - first) * 16, v.shape[0])
+        r = iota(shape, 0)
+        p = ((r >> 4) + first) * TOK + (r & 15) - base
+        fit = (iota(shape, 1) == p) & ((r & 15) < TOK)
+        placed = dot(jnp.where(fit, 1.0, 0.0).astype(BF), v).astype(BF)
+        rsend[first:end] = placed.reshape(end - first, 16, LANE)
+        for d in z_order[::-1]:
+            if first <= place_of(d) < end:
+                rzcopy(d).start()
+
+    for g in (1, 0):
+        at = pl.ds(bases[g], counts[g])
+        for d in far_first[:NY - 1]:
+            rycopy(g, d).wait_recv()
+            accs[g] = accs[g] + yrecv[d, at, :].astype(F32)
+        accs[g] = sealed(accs[g], counts[g])
+        if g:
+            send_back(accs[1], 64, 6, NZ)
+    send_back(jnp.concatenate(accs, axis=0), 0, 0, 6)
+    rrecv[z] = rsend[0]
 
     for d in z_order:
         rzcopy(d).wait_recv()
@@ -377,15 +405,15 @@
         cp.wait_send()
     for d in range(NY):
         if d:
-            rycopy(d).wait_send()
             for g in (0, 1):
+                rycopy(g, d).wait_send()
                 ycopy(g, d).wait_send()
         for way in (0, 1):
             for g in (0, 1):
                 x1copy(g, d, way).wait_send()
                 x2copy(g, d, way).wait_send()
-            s1copy(d, way).wait_send()
-            s2copy(d, way).wait_send()
+                s1copy(g, d, way).wait_send()
+                s2copy(g, d, way).wait_send()
 
 
 def body(tokens, out_grad, expert_ids, gate_probs, w_gate, w_up, w_down):
@@ -434,9 +462,9 @@
             dma((2, NY)), dma((2, NY)),
             dma((2, NY, 2)), dma((2, NY, 2)),
             dma((2, NY, 2)), dma((2, NY, 2)),
-            dma((NY, 2)), dma((NY, 2)),
-            dma((NY, 2)), dma((NY, 2)),
-            dma((NY,)), dma((NY,)),
+            dma((2, NY, 2)), dma((2, NY, 2)),
+            dma((2, NY, 2)), dma((2, NY, 2)),
+            dma((2, NY)), dma((2, NY)),
             dma((NZ,)), dma((NZ,)),
         ],
         compiler_params=pltpu.CompilerParams(

time: 89.2 us -> 88.6 us (level)
  no operation moved by 1% of the time
where the time goes in v4:
time: 88.6 us; the launch traced here: 86.9 us
  Pallas kernels  83.7 us (94%)
  local copies, waits for them, and re-layouts  2.5 us (3%)
    pallas_call x1, Pallas kernels, body(): pl.pallas_call(kernel, out_shape=(jax.ShapeDtypeStruct((TOK, FEAT), BF),...  83.7 us
    unnamed x2, local copies, waits for them, and re-layouts  2.5 us

profile of v4, /device:TPU:6, one launch (start us, length us, event | category | flops | bytes accessed | tf_op | source)
XLA Modules:
  0.0 86.9 jit_solution(3400203814645672245)
XLA Ops:
  0.6 83.7 %shard_map.86 = (bf16[12,96]{1,0:T(8,128)(2,1)}, f32[4,12]{1,0:T(4,128)}) custom-call(bf16[12,96]{1,0:T(8,128)(2,1)} %tok.1, bf16[12,96]{1,0:T(8,128)(2,1)} %grad.1, s32[4,12]{1,0:T(4,128)} %bitcast.3, f32[4,12]{1,0:T(4,128)} %bitcast.4, bf16[1,84,6144]{2,1,0:T(8,128)(2,1)} %wg.1, bf16[1,84,6144]{2,1,0:T(8,128)(2,1)} %wu.1, bf16[1,84,6144]{2,1,0:T(8,128)(2,1)} %wd.1), custom_call_target="tpu_custom_call" | custom-call | tf_op jit(solution)/shard_map/pallas_call | solution.py:423
  84.4 1.3 %copy.11 = bf16[12,96]{1,0:T(8,128)(2,1)} copy(bf16[12,96]{1,0:T(8,128)(2,1)} %get-tuple-element.8) | data formatting | bytes 4608
  85.6 1.2 %copy.12 = f32[12,4]{0,1:T(4,128)} copy(f32[12,4]{0,1:T(4,128)} %bitcast.5) | data formatting | bytes 384
